TPU v7x, 256 devices: a whole 4x4x8 slice. The times are simulated.
256 devices in a mesh: gx: 4 (over x), gy: 8 (over z), gz: 8 (over y, core).
Axes of the slice: x: 4, y: 4, z: 8, core: 2. Of those that a mesh axis runs over, the one named last changes fastest.
Arguments:
- solution: float32 [4, 8, 32, 64, 1024], P(None, None, 'gx', 'gy', 'gz'), may hold values from -6 to 6
- residual: float32 [4, 8, 32, 64, 1024], P(None, None, 'gx', 'gy', 'gz'), may hold values from -21 to 21
- permeability: float32 [4, 32, 64, 1024], P(None, 'gx', 'gy', 'gz'), may hold values from 0.1 to 1
- storage: float32 [4, 32, 64, 1024], P(None, 'gx', 'gy', 'gz'), may hold values from 0.5 to 2
- tissue_mask: int32 [32, 64, 1024], P('gx', 'gy', 'gz'), may hold values 0 or 1
- tissue_label: int32 [32, 64, 1024], P('gx', 'gy', 'gz'), may hold values from 0 to 2
- exchange_table: float32 [3, 6], replicated, may hold values from 0.2 to 1
Outputs:
- new_solution: float32 [4, 8, 32, 64, 1024], P(None, None, 'gx', 'gy', 'gz')
- new_residual: float32 [4, 8, 32, 64, 1024], P(None, None, 'gx', 'gy', 'gz')
- basis: float32 [4, 32, 32, 64, 1024], P(None, None, 'gx', 'gy', 'gz')
All inputs are finite; a program needn't handle non-finite values. No bound on the sum of `tissue_mask` on one device may be relied on, other than what follows from the above.
Results may differ from a plain program's by a relative error of at most 0.027.
Values sent between devices are 32-bit elements; how exact they have to be, the bound alone decides.
No kernel may reach another device: no remote copies, remote signals or barrier semaphores. Data moves between devices by JAX's collectives and lax.ppermute only.
A program may use at most 128 MiB of HBM per device.

v0:
```python
import jax
import jax.numpy as jnp
import numpy as np
from jax import lax
from jax.sharding import PartitionSpec as P

RHS = 8
S = 4
PAIRS = ((0, 1), (0, 2), (0, 3), (1, 2), (1, 3), (2, 3))
SHIFTS = (2.0, 14.0, 6.0, 10.0)
NEWTON_SCALE = 8.0
HIGHEST_PRECISION = lax.Precision.HIGHEST


def padded(cells, sides, width):
    for axis, dim in sides:
        count = lax.axis_size(axis)
        ends = count - 1
        head = lax.slice_in_dim(cells, 0, width, axis=dim)
        tail = lax.slice_in_dim(cells, cells.shape[dim] - width, cells.shape[dim], axis=dim)
        cells = jnp.concatenate(
            [
                lax.ppermute(tail, axis, [(i, (i + 1) % count) for i in range(ends)]),
                cells,
                lax.ppermute(head, axis, [((i + 1) % count, i) for i in range(ends)]),
            ],
            axis=dim,
        )
    return cells


def shifted(array, direction, offset):
    leading = array.ndim - 3
    index = [slice(None)] * leading
    for dimension in range(3):
        length = array.shape[leading + dimension]
        if dimension == direction:
            index.append(slice(offset, length - 2 + offset))
        else:
            index.append(slice(1, length - 1))
    return array[tuple(index)]


def interior(array):
    return shifted(array, 0, 1)


def stencil(field, perm_pad, mask_pad, store_pad, rate_pad):
    centre = interior(field)
    perm_mid = interior(perm_pad)
    mask_mid = interior(mask_pad)
    result = interior(store_pad)[:, None] * centre
    for direction in range(3):
        for offset in (0, 2):
            faces = (
                0.5
                * (perm_mid + shifted(perm_pad, direction, offset))
                * (mask_mid * shifted(mask_pad, direction, offset))
            )
            result = result + faces[:, None] * (centre - shifted(field, direction, offset))
    rate_mid = interior(rate_pad)
    pieces = [result[number] for number in range(4)]
    for number, pair in enumerate(PAIRS):
        flow = rate_mid[number] * (centre[pair[0]] - centre[pair[1]])
        pieces[pair[0]] = pieces[pair[0]] + flow
        pieces[pair[1]] = pieces[pair[1]] - flow
    return jnp.stack(pieces)


def apply_padded(field_pad, coeff_pad):
    return stencil(field_pad, coeff_pad[0:4], coeff_pad[14], coeff_pad[4:8], coeff_pad[8:14])


def build_coefficients(permeability, storage, tissue_mask, tissue_label, exchange_table):
    mask_float = tissue_mask.astype(jnp.float32)
    rates = jnp.zeros((6,) + tissue_mask.shape, jnp.float32)
    for level in range(3):
        weight = (tissue_label == level).astype(jnp.float32)
        rates = rates + exchange_table[level][:, None, None, None] * weight[None]
    rates = rates * mask_float[None]
    return jnp.concatenate([permeability, storage, rates, mask_float[None]], 0)


def newton_table(steps, rhs_count):
    table = np.zeros(((steps + 1) * rhs_count, steps * rhs_count), np.float32)
    for index in range(steps):
        table[
            index * rhs_count : (index + 1) * rhs_count, index * rhs_count : (index + 1) * rhs_count
        ] = SHIFTS[index] * np.eye(rhs_count)
        table[
            (index + 1) * rhs_count : (index + 2) * rhs_count,
            index * rhs_count : (index + 1) * rhs_count,
        ] = NEWTON_SCALE * np.eye(rhs_count)
    return jnp.asarray(table)


def local_gram(blocks):
    stacked = jnp.stack(blocks)
    flat = stacked.reshape(stacked.shape[0], stacked.shape[1], stacked.shape[2], -1)
    gram = jnp.einsum("kcjm,lcim->kjli", flat, flat, precision=HIGHEST_PRECISION)
    total = stacked.shape[0] * stacked.shape[2]
    return gram.reshape(total, total)


def lower_factor(matrix):
    extent = matrix.shape[0]
    positions = jnp.arange(extent)
    columns = []
    for col_index in range(extent):
        column = matrix[:, col_index]
        for inner in range(col_index):
            column = column - columns[inner] * columns[inner][col_index]
        pivot_value = jnp.sqrt(column[col_index])
        column = jnp.where(positions >= col_index, column / pivot_value, jnp.zeros_like(column))
        columns.append(column)
    return jnp.stack(columns, 1)


def lower_inverse(lower):
    extent = lower.shape[0]
    identity = jnp.eye(extent, dtype=lower.dtype)
    solved_rows = []
    for row_index in range(extent):
        current_row = identity[row_index]
        for inner in range(row_index):
            current_row = current_row - lower[row_index, inner] * solved_rows[inner]
        solved_rows.append(current_row / lower[row_index, row_index])
    return jnp.stack(solved_rows, 0)


def matmul(left, right):
    return jnp.dot(left, right, precision=HIGHEST_PRECISION)


def project(gram, steps, rhs_count):
    width = steps * rhs_count
    table = newton_table(steps, rhs_count)
    leading = gram[:width, :width]
    leading = 0.5 * (leading + leading.T)
    lower_inv = lower_inverse(lower_factor(leading))
    moment = matmul(gram[:width, :], table)
    moment = 0.5 * (moment + moment.T)
    projected = matmul(matmul(lower_inv, moment), lower_inv.T)
    projected = 0.5 * (projected + projected.T)
    right_part = matmul(lower_inv, gram[:width, :rhs_count])
    proj_inv = lower_inverse(lower_factor(projected))
    solved = matmul(proj_inv.T, matmul(proj_inv, right_part))
    inverse = lower_inv.T
    coeff = matmul(inverse, solved)
    extended = matmul(table, coeff)
    return (inverse, coeff, extended)


def finish(solution, residual, blocks, inverse, coeff, extended, steps, rhs_count):
    stacked = jnp.stack(blocks)
    flat = stacked.reshape(stacked.shape[0], stacked.shape[1], stacked.shape[2], -1)
    basis = jnp.einsum(
        "kcjm,kjq->cqm",
        flat[:steps],
        inverse.reshape(steps, rhs_count, -1),
        precision=HIGHEST_PRECISION,
    )
    basis = basis.reshape((stacked.shape[1], steps * rhs_count) + stacked.shape[3:])
    update = jnp.einsum(
        "kcjm,kji->cim",
        flat[:steps],
        coeff.reshape(steps, rhs_count, rhs_count),
        precision=HIGHEST_PRECISION,
    )
    image = jnp.einsum(
        "kcjm,kji->cim",
        flat,
        extended.reshape(steps + 1, rhs_count, rhs_count),
        precision=HIGHEST_PRECISION,
    )
    return (
        solution + update.reshape(solution.shape),
        residual - image.reshape(residual.shape),
        basis,
    )


def body(solution, residual, permeability, storage, tissue_mask, tissue_label, exchange_table):
    coefficients = build_coefficients(
        permeability, storage, tissue_mask, tissue_label, exchange_table
    )
    blocks = [residual]
    coeff_rim = padded(coefficients, (("gx", 1), ("gy", 2), ("gz", 3)), 1)
    current = residual
    for index in range(S):
        field_pad = padded(current, (("gx", 2), ("gy", 3), ("gz", 4)), 1)
        applied = apply_padded(field_pad, coeff_rim)
        current = (applied - SHIFTS[index] * current) / NEWTON_SCALE
        blocks.append(current)
    gram = lax.psum(local_gram(blocks), ("gx", "gy", "gz"))
    inverse, coeff, extended = project(gram, S, RHS)
    return finish(solution, residual, blocks, inverse, coeff, extended, S, RHS)


def solution(mesh):
    return jax.shard_map(
        body,
        mesh=mesh,
        in_specs=(
            P(None, None, "gx", "gy", "gz"),
            P(None, None, "gx", "gy", "gz"),
            P(None, "gx", "gy", "gz"),
            P(None, "gx", "gy", "gz"),
            P("gx", "gy", "gz"),
            P("gx", "gy", "gz"),
            P(),
        ),
        out_specs=(
            P(None, None, "gx", "gy", "gz"),
            P(None, None, "gx", "gy", "gz"),
            P(None, None, "gx", "gy", "gz"),
        ),
        check_vma=False,
    )
```

profile of v0, /device:TPU:1, one launch (start us, length us, event | category | flops | bytes accessed | tf_op | source)
XLA Modules:
  0.0 1804.4 jit_solution(12916086023873227692)
XLA Ops:
  157.0 5.2 collective-permute-start.20
  164.7 5.0 collective-permute-done.21
  182.9 6.5 collective-permute-start.22
  237.1 7.5 collective-permute-start.28
  262.7 8.3 fusion.4
  271.1 76.3 %psum.7 = f32[40,40]{1,0:T(8,128)S(1)} all-reduce(f32[40,40]{1,0:T(8,128)S(1)} %fusion.4), channel_id=1, replica_groups=mesh['gx'=4,'gy'=8,'gz'=8] {'gx','gy','gz'}, use_global_device_ids=true, to_apply=%region_0.0 | all-reduce | flops 1600 | bytes 12800 | tf_op jit(solution)/shard_map/psum | solution.py:195
  364.6 6.0 fusion.186
  404.2 5.7 multiply_subtract_fusion.51
  412.0 6.2 multiply_subtract_fusion.50
  420.2 6.8 multiply_subtract_fusion.49
  432.8 7.5 multiply_subtract_fusion.48
  442.4 6.1 fusion.177
  448.5 8.1 multiply_subtract_fusion.47
  458.7 8.7 multiply_subtract_fusion.46
  469.3 9.5 multiply_subtract_fusion.45
  480.9 9.6 multiply_subtract_fusion.44
  492.6 10.8 multiply_subtract_fusion.43
  505.4 10.9 multiply_subtract_fusion.42
  518.4 11.8 multiply_subtract_fusion.41
  532.2 12.5 multiply_subtract_fusion.40
  546.7 12.9 multiply_subtract_fusion.39
  561.5 6.0 fusion.168
  567.5 13.7 multiply_subtract_fusion.38
  583.1 14.4 multiply_subtract_fusion.37
  599.6 14.9 multiply_subtract_fusion.36
  616.4 15.8 multiply_subtract_fusion.35
  634.2 16.6 multiply_subtract_fusion.34
  652.9 16.6 multiply_subtract_fusion.33
  671.4 17.2 multiply_subtract_fusion.32
  690.8 18.4 %multiply_subtract_fusion.31 = f32[32]{0:T(128)S(1)} fusion(f32[32]{0:T(128)S(1)} %get-tuple-element.34, f32[]{:T(128)} %bitcast.543, f32[]{:T(128)} %bitcast.542, f32[]{:T(128)} %bitcast.541, f32[]{:T(128)} %bitcast.540, f32[]{:T(128)} %bitcast.539, f32[]{:T(128)} %bitcast.538, f32[]{:T(128)} %bitcast.537, f32[]{:T(128)} %bitcast.536, f32[]{:T(128)} %bitcast.535, ...), kind=kLoop, calls=%fused_computation.604 | loop fusion | flops 4608 | bytes 4196 | tf_op jit(solution)/shard_map/sub | solution.py:112
  711.1 19.0 %multiply_subtract_fusion.30 = f32[32]{0:T(128)S(1)} fusion(f32[32]{0:T(128)S(1)} %get-tuple-element.33, f32[]{:T(128)} %bitcast.576, f32[]{:T(128)} %bitcast.575, f32[]{:T(128)} %bitcast.574, f32[]{:T(128)} %bitcast.573, f32[]{:T(128)} %bitcast.572, f32[]{:T(128)} %bitcast.571, f32[]{:T(128)} %bitcast.570, f32[]{:T(128)} %bitcast.569, f32[]{:T(128)} %bitcast.568, ...), kind=kLoop, calls=%fused_computation.602 | loop fusion | flops 4768 | bytes 4332 | tf_op jit(solution)/shard_map/sub | solution.py:112
  731.9 65.1 %subtract_divide_fusion.49 = (f32[1,32]{1,0:T(1,128)S(1)}, f32[1,32]{1,0:T(1,128)S(1)}, f32[1,32]{1,0:T(1,128)S(1)}, f32[1,32]{1,0:T(1,128)S(1)}, f32[1,32]{1,0:...) fusion(f32[32,32]{1,0:T(8,128)S(1)} %fusion.206, ...), kind=kLoop, calls=%fused_computation.639 | loop fusion | flops 6272 | bytes 4004 | tf_op jit(solution)/shard_map/div | solution.py:127
  797.1 137.1 %subtract_divide_fusion.38 = (f32[1,32]{1,0:T(1,128)S(1)}, f32[1,32]{1,0:T(1,128)S(1)}, f32[1,32]{1,0:T(1,128)S(1)}, f32[1,32]{1,0:T(1,128)S(1)}, f32[1,32]{1,0:...) fusion(f32[1,32]{1,0:T(1,128)S(1)} %get-tuple-element.113, ...), kind=kLoop, calls=%fused_computation.617 | loop fusion | flops 13728 | bytes 5488 | tf_op jit(solution)/shard_map/div | solution.py:127
  934.2 127.1 %subtract_divide_fusion.31 = (f32[1,32]{1,0:T(1,128)S(1)}, f32[1,32]{1,0:T(1,128)S(1)}, f32[1,32]{1,0:T(1,128)S(1)}, f32[1,32]{1,0:T(1,128)S(1)}, f32[1,32]{1,0:...) fusion(f32[1,32]{1,0:T(1,128)S(1)} %get-tuple-element.102, f32[1,32]{1,0:T(1,128)S(1)} %get-tuple-element.103, ...), kind=kLoop, calls=%fused_computation.603 | loop fusion | flops 12768 | bytes 5804 | tf_op jit(solution)/shard_map/div | solution.py:127
  1079.1 6.2 fusion.154
  1118.9 5.7 multiply_subtract_fusion.21
  1126.6 6.2 multiply_subtract_fusion.20
  1134.9 6.8 multiply_subtract_fusion.19
  1147.2 7.4 multiply_subtract_fusion.18
  1156.8 6.1 fusion.145
  1162.9 8.1 multiply_subtract_fusion.17
  1173.1 8.7 multiply_subtract_fusion.16
  1183.7 9.5 multiply_subtract_fusion.15
  1195.3 9.6 multiply_subtract_fusion.14
  1207.0 10.8 multiply_subtract_fusion.13
  1219.8 10.9 multiply_subtract_fusion.12
  1232.8 11.8 multiply_subtract_fusion.11
  1246.6 12.5 multiply_subtract_fusion.10
  1261.1 12.9 multiply_subtract_fusion.9
  1275.9 6.0 fusion.136
  1281.9 13.7 multiply_subtract_fusion.8
  1297.5 14.4 multiply_subtract_fusion.7
  1314.0 14.9 multiply_subtract_fusion.6
  1330.8 15.8 multiply_subtract_fusion.5
  1348.7 16.6 multiply_subtract_fusion.4
  1367.3 16.6 multiply_subtract_fusion.3
  1385.8 17.2 multiply_subtract_fusion.2
  1405.2 18.4 %multiply_subtract_fusion.1 = f32[32]{0:T(128)S(1)} fusion(f32[32]{0:T(128)S(1)} %get-tuple-element.4, f32[]{:T(128)} %bitcast.1105, f32[]{:T(128)} %bitcast.1104, f32[]{:T(128)} %bitcast.1103, f32[]{:T(128)} %bitcast.1102, f32[]{:T(128)} %bitcast.1101, f32[]{:T(128)} %bitcast.1100, f32[]{:T(128)} %bitcast.1099, f32[]{:T(128)} %bitcast.1098, f32[]{:T(128)} %bitcast.1097, ...), kind=kLoop, calls=%fused_computation.543 | loop fusion | flops 4608 | bytes 4196 | tf_op jit(solution)/shard_map/sub | solution.py:112
  1425.5 19.0 %multiply_subtract_fusion = f32[32]{0:T(128)S(1)} fusion(f32[32]{0:T(128)S(1)} %get-tuple-element.3, f32[]{:T(128)} %bitcast.1138, f32[]{:T(128)} %bitcast.1137, f32[]{:T(128)} %bitcast.1136, f32[]{:T(128)} %bitcast.1135, f32[]{:T(128)} %bitcast.1134, f32[]{:T(128)} %bitcast.1133, f32[]{:T(128)} %bitcast.1132, f32[]{:T(128)} %bitcast.1131, f32[]{:T(128)} %bitcast.1130, ...), kind=kLoop, calls=%fused_computation.541 | loop fusion | flops 4768 | bytes 4332 | tf_op jit(solution)/shard_map/sub | solution.py:112
  1446.3 65.1 %subtract_divide_fusion.18 = (f32[1,32]{1,0:T(1,128)S(1)}, f32[1,32]{1,0:T(1,128)S(1)}, f32[1,32]{1,0:T(1,128)S(1)}, f32[1,32]{1,0:T(1,128)S(1)}, f32[1,32]{1,0:...) fusion(f32[32,32]{1,0:T(8,128)S(1)} %fusion.206, ...), kind=kLoop, calls=%fused_computation.578 | loop fusion | flops 6272 | bytes 4004 | tf_op jit(solution)/shard_map/div | solution.py:127
  1511.5 137.1 %subtract_divide_fusion.7 = (f32[1,32]{1,0:T(1,128)S(1)}, f32[1,32]{1,0:T(1,128)S(1)}, f32[1,32]{1,0:T(1,128)S(1)}, f32[1,32]{1,0:T(1,128)S(1)}, f32[1,32]{1,0:T...) fusion(f32[1,32]{1,0:T(1,128)S(1)} %get-tuple-element.81, ...), kind=kLoop, calls=%fused_computation.556 | loop fusion | flops 13728 | bytes 5488 | tf_op jit(solution)/shard_map/div | solution.py:127
  1648.6 127.1 %subtract_divide_fusion = (f32[1,32]{1,0:T(1,128)S(1)}, f32[1,32]{1,0:T(1,128)S(1)}, f32[1,32]{1,0:T(1,128)S(1)}, f32[1,32]{1,0:T(1,128)S(1)}, f32[1,32]{1,0:T(1...) fusion(f32[1,32]{1,0:T(1,128)S(1)} %get-tuple-element.70, f32[1,32]{1,0:T(1,128)S(1)} %get-tuple-element.71, ...), kind=kLoop, calls=%fused_computation.542 | loop fusion | flops 12768 | bytes 5804 | tf_op jit(solution)/shard_map/div | solution.py:127
  1776.6 11.7 fusion.131
  1788.3 7.5 fusion.3
  (555 shorter events, 399.2 us)
Async XLA Ops:
  0.6 8.7 copy-start
  2.2 55.6 %copy-start.49 = (f32[1,8,8,128]{3,2,1,0:T(8,128)}, f32[1,8,8,128]{3,2,1,0:T(8,128)S(1)}, u32[]{:S(2)}) copy-start(f32[1,8,8,128]{3,2,1,0:T(8,128)S(1)} %get-tuple-element.202) | copy-start | bytes 98308
  3.9 12.6 copy-start.9
  3.9 12.6 copy-start.10
  3.9 17.9 collective-permute-start
  8.0 13.8 collective-permute-start.1
  10.0 18.1 %collective-permute-start.7 = (f32[4,8,1,8,128]{4,1,3,2,0:T(8,128)S(1)}, f32[4,8,1,8,128]{4,1,3,2,0:T(8,128)S(1)}, u32[]{:S(2)}, u32[]{:S(2)}) collective-permute-start(f32[4,8,1,8,128]{4,1,3,2,0:T(8,128)S(1)} %get-tuple-element.169), channel_id=1, source_target_pairs={{64,0},{128,64},{192,128},{65,1},{129,65},{193,129},{66,2},{130,66... | collective-permute-start | bytes 393224 | tf_op jit(solution)/shard_map/ppermute | solution.py:25
  11.3 16.1 collective-permute-start.6
  16.6 74.7 %copy-start.32 = (f32[8,8,128]{2,1,0:T(8,128)}, f32[8,8,128]{2,1,0:T(8,128)S(1)}, u32[]{:S(2)}) copy-start(f32[8,8,128]{2,1,0:T(8,128)S(1)} %get-tuple-element.183) | copy-start | bytes 98308
  16.6 74.7 %copy-start.36 = (f32[8,8,128]{2,1,0:T(8,128)}, f32[8,8,128]{2,1,0:T(8,128)S(1)}, u32[]{:S(2)}) copy-start(f32[8,8,128]{2,1,0:T(8,128)S(1)} %get-tuple-element.184) | copy-start | bytes 98308
  16.6 74.7 %copy-start.40 = (f32[8,8,128]{2,1,0:T(8,128)}, f32[8,8,128]{2,1,0:T(8,128)S(1)}, u32[]{:S(2)}) copy-start(f32[8,8,128]{2,1,0:T(8,128)S(1)} %get-tuple-element.185) | copy-start | bytes 98308
  16.6 74.7 %copy-start.44 = (f32[8,8,128]{2,1,0:T(8,128)}, f32[8,8,128]{2,1,0:T(8,128)S(1)}, u32[]{:S(2)}) copy-start(f32[8,8,128]{2,1,0:T(8,128)S(1)} %get-tuple-element.188) | copy-start | bytes 98308
  21.8 36.0 %copy-start.48 = (f32[15,1,8,128]{3,2,1,0:T(8,128)}, f32[15,1,8,128]{3,2,1,0:T(8,128)S(1)}, u32[]{:S(2)}) copy-start(f32[15,1,8,128]{3,2,1,0:T(8,128)S(1)} %collective-permute-done.1) | copy-start | bytes 184324
  21.9 6.2 collective-permute-start.3
  23.2 5.6 collective-permute-start.2
  28.2 29.6 %copy-start.50 = (f32[15,10,1,128]{3,2,1,0:T(1,128)}, f32[15,10,1,128]{3,2,1,0:T(1,128)S(1)}, u32[]{:S(2)}) copy-start(f32[15,10,1,128]{3,2,1,0:T(1,128)S(1)} %copy.194) | copy-start | bytes 230404
  29.3 25.8 %copy-start.51 = (f32[15,10,1,128]{3,2,1,0:T(1,128)}, f32[15,10,1,128]{3,2,1,0:T(1,128)S(1)}, u32[]{:S(2)}) copy-start(f32[15,10,1,128]{3,2,1,0:T(1,128)S(1)} %copy.193) | copy-start | bytes 230404
  36.0 17.0 collective-permute-start.5
  40.1 10.8 collective-permute-start.4
  44.9 14.5 collective-permute-start.8
  49.6 9.8 collective-permute-start.9
  57.8 29.5 %copy-start.30 = (f32[4,8,8,128]{3,2,1,0:T(8,128)}, f32[4,8,8,128]{3,2,1,0:T(8,128)S(1)}, u32[]{:S(2)}) copy-start(f32[4,8,8,128]{3,2,1,0:T(8,128)S(1)} %get-tuple-element.175) | copy-start | bytes 393220
  57.8 29.5 %copy-start.31 = (f32[4,8,8,128]{3,2,1,0:T(8,128)}, f32[4,8,8,128]{3,2,1,0:T(8,128)S(1)}, u32[]{:S(2)}) copy-start(f32[4,8,8,128]{3,2,1,0:T(8,128)S(1)} %get-tuple-element.176) | copy-start | bytes 393220
  59.4 27.9 %copy-start.25 = (f32[4,8,8,128]{3,2,1,0:T(8,128)}, f32[4,8,8,128]{3,2,1,0:T(8,128)S(1)}, u32[]{:S(2)}) copy-start(f32[4,8,8,128]{3,2,1,0:T(8,128)S(1)} %get-tuple-element.182) | copy-start | bytes 393220
  71.0 12.2 collective-permute-start.11
  73.0 6.2 collective-permute-start.10
  78.0 9.3 copy-start.27
  78.0 9.3 copy-start.29
  78.0 9.3 copy-start.74
  78.0 9.3 copy-start.76
  92.8 5.8 collective-permute-start.12
  96.5 6.3 collective-permute-start.13
  98.7 16.6 copy-start.55
  102.8 12.5 copy-start.57
  102.8 7.7 collective-permute-start.14
  106.8 8.3 collective-permute-start.15
  110.5 4.7 copy-start.70
  121.4 9.9 collective-permute-start.16
  129.4 6.6 collective-permute-start.17
  139.2 4.3 copy-start.45
  139.2 4.3 copy-start.64
  147.9 5.8 collective-permute-start.18
  151.0 5.9 collective-permute-start.19
  153.6 9.9 copy-start.7
  153.6 16.1 copy-start.54
  156.9 12.8 copy-start.56
  157.0 7.8 collective-permute-start.20
  162.2 7.6 collective-permute-start.21
  164.7 5.0 copy-start.69
  180.9 15.0 collective-permute-start.23
  182.9 9.0 collective-permute-start.22
  189.4 10.7 copy-start.2
  189.4 10.7 copy-start.26
  189.4 10.7 copy-start.28
  205.7 3.9 collective-permute-start.24
  207.3 5.7 collective-permute-start.25
  209.6 14.3 copy-start.52
  213.0 11.0 copy-start.53
  213.0 7.2 collective-permute-start.26
  217.9 6.1 collective-permute-start.27
  235.1 15.8 collective-permute-start.29
  237.1 9.8 collective-permute-start.28
  262.7 169.8 %copy-start.77 = (f32[40,32]{1,0:T(8,128)S(1)}, f32[40,32]{1,0:T(8,128)}, u32[]{:S(2)}) copy-start(f32[40,32]{1,0:T(8,128)} %constant.92.clone) | copy-start | bytes 15364
  1776.6 11.7 copy-start.8
  (44 other events, 98.0 us)
where the time goes:
time: 1830 us; the launch traced here: 1800 us
  other arithmetic  1320 us (72%)
  local copies, waits for them, and re-layouts  207 us (11%)
  starting transfers between devices  90.5 us (5%)
  blocking collectives  76.3 us (4%)
  between operations  47.1 us (3%)
  waiting for transfers between devices  34.7 us (2%)
  matrix products  32.4 us (2%)
    div x6, other arithmetic, lower_inverse(): solved_rows.append(current_row / lower[row_index, row_index])  659 us
    sub x68, other arithmetic, lower_factor(): column = column - columns[inner] * columns[inner][col_index]  621 us
    psum x1, blocking collectives, body(): gram = lax.psum(local_gram(blocks), ('gx', 'gy', 'gz'))  76.3 us
    ppermute x15, starting transfers between devices, padded(): lax.ppermute(tail, axis, [(i, (i + 1) % count) for i in range(ends)])  65.7 us
    slice x64, local copies, waits for them, and re-layouts, lower_factor(): pivot_value = jnp.sqrt(column[col_index])  39.9 us
    slice x54, local copies, waits for them, and re-layouts, lower_inverse(): current_row = current_row - lower[row_index, inner] * solved_rows[inner]  38.3 us
  transfers between devices with their start and end apart: 30, of which 14 were waited for; matrix products, arithmetic and copies ran while one was open for 2% of the time, Pallas kernels for 0%

commit v1 on v0

--- a/solution.py
+++ b/solution.py
@@ -192,7 +192,7 @@
         applied = apply_padded(field_pad, coeff_rim)
         current = (applied - SHIFTS[index] * current) / NEWTON_SCALE
         blocks.append(current)
-    gram = lax.psum(local_gram(blocks), ("gx", "gy", "gz"))
+    gram = lax.psum(lax.psum(local_gram(blocks), ("gy", "gz")), "gx")
     inverse, coeff, extended = project(gram, S, RHS)
     return finish(solution, residual, blocks, inverse, coeff, extended, S, RHS)
 

time: 1830 us -> 2010 us (1.098)
  blocking collectives: 76.3 us -> 252 us
    psum x1 -> x2, blocking collectives: 76.3 us -> 252 us  [body(): gram = lax.psum(lax.psum(local_gram(blocks), ('gy', 'gz')), 'gx')]
where the time goes in v1:
time: 2010 us; the launch traced here: 1980 us
  other arithmetic  1320 us (66%)
  blocking collectives  252 us (13%)
  local copies, waits for them, and re-layouts  207 us (10%)
  starting transfers between devices  90.4 us (4%)
  between operations  47.2 us (2%)
  waiting for transfers between devices  34.7 us (2%)
  matrix products  32.4 us (2%)
    div x6, other arithmetic, lower_inverse(): solved_rows.append(current_row / lower[row_index, row_index])  659 us
    sub x68, other arithmetic, lower_factor(): column = column - columns[inner] * columns[inner][col_index]  621 us
    psum x2, blocking collectives, body(): gram = lax.psum(lax.psum(local_gram(blocks), ('gy', 'gz')), 'gx')  252 us
    ppermute x15, starting transfers between devices, padded(): lax.ppermute(tail, axis, [(i, (i + 1) % count) for i in range(ends)])  65.7 us
  transfers between devices with their start and end apart: 30, of which 14 were waited for; matrix products, arithmetic and copies ran while one was open for 2% of the time, Pallas kernels for 0%

profile of v1, /device:TPU:1, one launch (start us, length us, event | category | flops | bytes accessed | tf_op | source)
XLA Modules:
  0.0 1980.2 jit_solution(7008119767997113431)
XLA Ops:
  156.9 5.2 collective-permute-start.20
  182.8 6.4 collective-permute-start.22
  237.1 7.5 collective-permute-start.28
  262.8 8.3 fusion.4
  271.1 241.0 %psum.14 = f32[40,40]{1,0:T(8,128)S(1)} all-reduce(f32[40,40]{1,0:T(8,128)S(1)} %fusion.4), channel_id=1, replica_groups=mesh['gx'=4,'gy'=8,'gz'=8] {'gy','gz'}, use_global_device_ids=true, to_apply=%region_0.0 | all-reduce | flops 1600 | bytes 12800 | tf_op jit(solution)/shard_map/psum | solution.py:195
  512.1 11.3 psum.15
  540.5 5.8 fusion.186
  580.3 5.4 multiply_subtract_fusion.51
  587.8 6.3 multiply_subtract_fusion.50
  596.2 6.8 multiply_subtract_fusion.49
  608.6 7.6 multiply_subtract_fusion.48
  618.3 6.1 fusion.177
  624.3 7.8 multiply_subtract_fusion.47
  634.3 8.8 multiply_subtract_fusion.46
  645.1 9.0 multiply_subtract_fusion.45
  656.3 9.9 multiply_subtract_fusion.44
  668.3 10.7 multiply_subtract_fusion.43
  680.9 11.1 multiply_subtract_fusion.42
  694.0 11.8 multiply_subtract_fusion.41
  707.9 12.6 multiply_subtract_fusion.40
  722.5 13.1 multiply_subtract_fusion.39
  737.8 5.9 fusion.168
  743.7 13.8 multiply_subtract_fusion.38
  759.6 14.7 multiply_subtract_fusion.37
  776.2 14.8 multiply_subtract_fusion.36
  792.9 15.4 multiply_subtract_fusion.35
  810.3 16.5 multiply_subtract_fusion.34
  828.8 16.9 multiply_subtract_fusion.33
  847.5 17.4 multiply_subtract_fusion.32
  866.9 18.2 multiply_subtract_fusion.31
  887.2 18.9 multiply_subtract_fusion.30
  907.9 65.3 %subtract_divide_fusion.49 = (f32[1,32]{1,0:T(1,128)S(1)}, f32[1,32]{1,0:T(1,128)S(1)}, f32[1,32]{1,0:T(1,128)S(1)}, f32[1,32]{1,0:T(1,128)S(1)}, f32[1,32]{1,0:...) fusion(f32[32,32]{1,0:T(8,128)S(1)} %fusion.206, ...), kind=kLoop, calls=%fused_computation.639 | loop fusion | flops 6272 | bytes 4004 | tf_op jit(solution)/shard_map/div | solution.py:127
  973.2 137.1 %subtract_divide_fusion.38 = (f32[1,32]{1,0:T(1,128)S(1)}, f32[1,32]{1,0:T(1,128)S(1)}, f32[1,32]{1,0:T(1,128)S(1)}, f32[1,32]{1,0:T(1,128)S(1)}, f32[1,32]{1,0:...) fusion(f32[1,32]{1,0:T(1,128)S(1)} %get-tuple-element.113, ...), kind=kLoop, calls=%fused_computation.617 | loop fusion | flops 13728 | bytes 5488 | tf_op jit(solution)/shard_map/div | solution.py:127
  1110.3 126.8 %subtract_divide_fusion.31 = (f32[1,32]{1,0:T(1,128)S(1)}, f32[1,32]{1,0:T(1,128)S(1)}, f32[1,32]{1,0:T(1,128)S(1)}, f32[1,32]{1,0:T(1,128)S(1)}, f32[1,32]{1,0:...) fusion(f32[1,32]{1,0:T(1,128)S(1)} %get-tuple-element.102, f32[1,32]{1,0:T(1,128)S(1)} %get-tuple-element.103, ...), kind=kLoop, calls=%fused_computation.603 | loop fusion | flops 12768 | bytes 5804 | tf_op jit(solution)/shard_map/div | solution.py:127
  1254.9 6.0 fusion.154
  1294.8 5.4 multiply_subtract_fusion.21
  1302.4 6.3 multiply_subtract_fusion.20
  1310.7 6.8 multiply_subtract_fusion.19
  1322.9 7.6 multiply_subtract_fusion.18
  1332.5 6.1 fusion.145
  1338.6 7.8 multiply_subtract_fusion.17
  1348.6 8.8 multiply_subtract_fusion.16
  1359.4 9.0 multiply_subtract_fusion.15
  1370.5 9.9 multiply_subtract_fusion.14
  1382.6 10.7 multiply_subtract_fusion.13
  1395.1 11.1 multiply_subtract_fusion.12
  1408.3 11.8 multiply_subtract_fusion.11
  1422.2 12.6 multiply_subtract_fusion.10
  1436.8 13.1 multiply_subtract_fusion.9
  1452.1 5.9 fusion.136
  1458.0 13.8 multiply_subtract_fusion.8
  1473.9 14.7 multiply_subtract_fusion.7
  1490.5 14.8 multiply_subtract_fusion.6
  1507.2 15.4 multiply_subtract_fusion.5
  1524.6 16.5 multiply_subtract_fusion.4
  1543.1 16.9 multiply_subtract_fusion.3
  1561.8 17.4 multiply_subtract_fusion.2
  1581.2 18.2 multiply_subtract_fusion.1
  1601.5 18.9 multiply_subtract_fusion
  1622.2 65.3 %subtract_divide_fusion.18 = (f32[1,32]{1,0:T(1,128)S(1)}, f32[1,32]{1,0:T(1,128)S(1)}, f32[1,32]{1,0:T(1,128)S(1)}, f32[1,32]{1,0:T(1,128)S(1)}, f32[1,32]{1,0:...) fusion(f32[32,32]{1,0:T(8,128)S(1)} %fusion.206, ...), kind=kLoop, calls=%fused_computation.578 | loop fusion | flops 6272 | bytes 4004 | tf_op jit(solution)/shard_map/div | solution.py:127
  1687.5 137.1 %subtract_divide_fusion.7 = (f32[1,32]{1,0:T(1,128)S(1)}, f32[1,32]{1,0:T(1,128)S(1)}, f32[1,32]{1,0:T(1,128)S(1)}, f32[1,32]{1,0:T(1,128)S(1)}, f32[1,32]{1,0:T...) fusion(f32[1,32]{1,0:T(1,128)S(1)} %get-tuple-element.81, ...), kind=kLoop, calls=%fused_computation.556 | loop fusion | flops 13728 | bytes 5488 | tf_op jit(solution)/shard_map/div | solution.py:127
  1824.6 126.8 %subtract_divide_fusion = (f32[1,32]{1,0:T(1,128)S(1)}, f32[1,32]{1,0:T(1,128)S(1)}, f32[1,32]{1,0:T(1,128)S(1)}, f32[1,32]{1,0:T(1,128)S(1)}, f32[1,32]{1,0:T(1...) fusion(f32[1,32]{1,0:T(1,128)S(1)} %get-tuple-element.70, f32[1,32]{1,0:T(1,128)S(1)} %get-tuple-element.71, ...), kind=kLoop, calls=%fused_computation.542 | loop fusion | flops 12768 | bytes 5804 | tf_op jit(solution)/shard_map/div | solution.py:127
  1952.4 11.7 fusion.131
  1964.1 7.5 fusion.3
  (556 shorter events, 404.5 us)
Async XLA Ops:
  0.6 8.7 copy-start
  2.2 55.6 %copy-start.49 = (f32[1,8,8,128]{3,2,1,0:T(8,128)}, f32[1,8,8,128]{3,2,1,0:T(8,128)S(1)}, u32[]{:S(2)}) copy-start(f32[1,8,8,128]{3,2,1,0:T(8,128)S(1)} %get-tuple-element.202) | copy-start | bytes 98308
  3.9 12.6 copy-start.9
  3.9 12.6 copy-start.10
  3.9 17.9 collective-permute-start
  8.0 13.8 collective-permute-start.1
  10.0 18.1 collective-permute-start.7
  11.3 16.1 collective-permute-start.6
  16.6 74.7 %copy-start.32 = (f32[8,8,128]{2,1,0:T(8,128)}, f32[8,8,128]{2,1,0:T(8,128)S(1)}, u32[]{:S(2)}) copy-start(f32[8,8,128]{2,1,0:T(8,128)S(1)} %get-tuple-element.183) | copy-start | bytes 98308
  16.6 74.7 %copy-start.36 = (f32[8,8,128]{2,1,0:T(8,128)}, f32[8,8,128]{2,1,0:T(8,128)S(1)}, u32[]{:S(2)}) copy-start(f32[8,8,128]{2,1,0:T(8,128)S(1)} %get-tuple-element.184) | copy-start | bytes 98308
  16.6 74.7 %copy-start.40 = (f32[8,8,128]{2,1,0:T(8,128)}, f32[8,8,128]{2,1,0:T(8,128)S(1)}, u32[]{:S(2)}) copy-start(f32[8,8,128]{2,1,0:T(8,128)S(1)} %get-tuple-element.185) | copy-start | bytes 98308
  16.6 74.7 %copy-start.44 = (f32[8,8,128]{2,1,0:T(8,128)}, f32[8,8,128]{2,1,0:T(8,128)S(1)}, u32[]{:S(2)}) copy-start(f32[8,8,128]{2,1,0:T(8,128)S(1)} %get-tuple-element.188) | copy-start | bytes 98308
  21.8 36.0 %copy-start.48 = (f32[15,1,8,128]{3,2,1,0:T(8,128)}, f32[15,1,8,128]{3,2,1,0:T(8,128)S(1)}, u32[]{:S(2)}) copy-start(f32[15,1,8,128]{3,2,1,0:T(8,128)S(1)} %collective-permute-done.1) | copy-start | bytes 184324
  21.9 6.2 collective-permute-start.3
  23.2 5.6 collective-permute-start.2
  28.2 29.6 %copy-start.50 = (f32[15,10,1,128]{3,2,1,0:T(1,128)}, f32[15,10,1,128]{3,2,1,0:T(1,128)S(1)}, u32[]{:S(2)}) copy-start(f32[15,10,1,128]{3,2,1,0:T(1,128)S(1)} %copy.194) | copy-start | bytes 230404
  29.3 25.8 %copy-start.51 = (f32[15,10,1,128]{3,2,1,0:T(1,128)}, f32[15,10,1,128]{3,2,1,0:T(1,128)S(1)}, u32[]{:S(2)}) copy-start(f32[15,10,1,128]{3,2,1,0:T(1,128)S(1)} %copy.193) | copy-start | bytes 230404
  36.0 16.9 collective-permute-start.5
  40.1 10.8 collective-permute-start.4
  44.9 14.4 collective-permute-start.8
  49.6 9.8 collective-permute-start.9
  57.8 29.4 %copy-start.30 = (f32[4,8,8,128]{3,2,1,0:T(8,128)}, f32[4,8,8,128]{3,2,1,0:T(8,128)S(1)}, u32[]{:S(2)}) copy-start(f32[4,8,8,128]{3,2,1,0:T(8,128)S(1)} %get-tuple-element.175) | copy-start | bytes 393220
  57.8 29.4 %copy-start.31 = (f32[4,8,8,128]{3,2,1,0:T(8,128)}, f32[4,8,8,128]{3,2,1,0:T(8,128)S(1)}, u32[]{:S(2)}) copy-start(f32[4,8,8,128]{3,2,1,0:T(8,128)S(1)} %get-tuple-element.176) | copy-start | bytes 393220
  59.4 27.9 %copy-start.25 = (f32[4,8,8,128]{3,2,1,0:T(8,128)}, f32[4,8,8,128]{3,2,1,0:T(8,128)S(1)}, u32[]{:S(2)}) copy-start(f32[4,8,8,128]{3,2,1,0:T(8,128)S(1)} %get-tuple-element.182) | copy-start | bytes 393220
  71.0 12.2 collective-permute-start.11
  72.9 6.2 collective-permute-start.10
  77.9 9.3 copy-start.27
  78.0 9.3 copy-start.29
  78.0 9.3 copy-start.74
  78.0 9.3 copy-start.76
  92.8 5.8 collective-permute-start.12
  96.4 6.3 collective-permute-start.13
  98.6 16.6 copy-start.55
  102.7 12.5 copy-start.57
  102.8 7.7 collective-permute-start.14
  106.8 8.3 collective-permute-start.15
  110.5 4.7 copy-start.70
  121.4 9.9 collective-permute-start.16
  129.4 6.6 collective-permute-start.17
  139.2 4.3 copy-start.45
  139.2 4.3 copy-start.64
  147.9 5.8 collective-permute-start.18
  151.0 5.9 collective-permute-start.19
  153.6 9.9 copy-start.7
  153.6 16.1 copy-start.54
  156.9 12.8 copy-start.56
  156.9 7.8 collective-permute-start.20
  162.2 7.6 collective-permute-start.21
  164.7 5.0 copy-start.69
  180.9 15.0 collective-permute-start.23
  182.8 9.0 collective-permute-start.22
  189.3 10.7 copy-start.2
  189.3 10.7 copy-start.26
  189.3 10.7 copy-start.28
  205.7 4.0 collective-permute-start.24
  207.3 5.7 collective-permute-start.25
  209.6 14.3 copy-start.52
  213.0 11.0 copy-start.53
  213.0 7.2 collective-permute-start.26
  217.9 6.1 collective-permute-start.27
  235.2 15.8 collective-permute-start.29
  237.1 9.8 collective-permute-start.28
  262.8 345.6 %copy-start.77 = (f32[40,32]{1,0:T(8,128)S(1)}, f32[40,32]{1,0:T(8,128)}, u32[]{:S(2)}) copy-start(f32[40,32]{1,0:T(8,128)} %constant.92.clone) | copy-start | bytes 15364
  1952.4 11.7 copy-start.8
  (44 other events, 98.0 us)
